TPU v7x, 32 devices: a whole 2x2x4 slice. The times are simulated.
32 devices in a mesh: grp: 4 (over y, x), docs: 8 (over z, core).
Axes of the slice: x: 2, y: 2, z: 4, core: 2. Of those that a mesh axis runs over, the one named last changes fastest.
Arguments:
- embeddings: float32 [131072, 1024], P(('grp', 'docs'))
- assign: int32 [131072], P(('grp', 'docs')), may hold values from 0 to 767, as said below
- cluster_slot: int32 [768], replicated, may hold values from 0 to 767, as said below
Outputs:
- centroids: float32 [768, 1024], P('docs')
- max_sim: float32 [131072], P(('grp', 'docs'))
- centroid_cos: float32 [131072], P(('grp', 'docs'))
Inputs may be any that keep to these rules, and one draw needn't show every extreme that they name: Each device's rows are ordered by owner, cluster_slot[assign] // 96; a device sends at most 640 rows to one owner and some device sends exactly 640; every owner receives exactly 4096 rows from the devices of its group; in each group every cluster is named by 2 to 128 rows, and some cluster by exactly 128. A permutation: cluster c is held at slot cluster_slot[c] by the owner of index cluster_slot[c] // 96 along docs.
All inputs are finite; a program needn't handle non-finite values.
Results may differ from a plain program's by a relative error of at most 0.0003.
Values may be sent and summed in bfloat16 or wider, within the bound.
No kernel may reach another device: no remote copies, remote signals or barrier semaphores. Data moves between devices by JAX's collectives and lax.ppermute only.
A program may use at most 192 MiB of HBM per device.

v0:
```python
import jax
import jax.numpy as jnp
from jax import lax
from jax.sharding import PartitionSpec as P

epsilon = 1e-06
highest = lax.Precision.HIGHEST


def unit_rows(values):
    return values * lax.rsqrt(jnp.sum(values * values, -1, keepdims=True) + epsilon)


def label_table(labels, cluster_range):
    return (labels[:, :, None] == cluster_range[None, None, :]).astype(jnp.float32)


def per_device(embeddings, assign, cluster_slot):
    row_count, feature_width = embeddings.shape
    owner_count = lax.axis_size("docs")
    cluster_count = cluster_slot.shape[0]
    per_owner = cluster_count // owner_count
    block_rows = 3 * row_count // per_owner
    capacity = row_count // owner_count + row_count // (4 * owner_count)
    slot_of_row = cluster_slot[assign]
    owner_of_row = slot_of_row // per_owner
    local_of_row = slot_of_row % per_owner
    owner_range = jnp.arange(owner_count, dtype=jnp.int32)
    send_counts = jnp.sum((owner_of_row[:, None] == owner_range[None, :]).astype(jnp.int32), 0)
    send_offsets = jnp.cumsum(send_counts) - send_counts
    slot_range = jnp.arange(capacity, dtype=jnp.int32)
    occupied = slot_range[None, :] < send_counts[:, None]
    source_row = jnp.where(occupied, send_offsets[:, None] + slot_range[None, :], 0)
    out_labels = jnp.where(occupied, local_of_row[source_row], per_owner)
    cluster_range = jnp.arange(per_owner, dtype=jnp.int32)
    gathered = jnp.where(occupied[:, :, None], embeddings[source_row], jnp.zeros((), jnp.float32))
    send_table = label_table(out_labels, cluster_range)
    partial_sums = jnp.einsum(
        "nck,ncd->nkd", send_table, gathered, precision=highest, preferred_element_type=jnp.float32
    ).reshape(cluster_count, feature_width)
    partial_tally = jnp.sum(send_table, 1).reshape(cluster_count)
    total_sums, total_tally = lax.psum((partial_sums, partial_tally), ("grp", "docs"))
    first_slot = lax.axis_index("docs") * per_owner
    owned_sums = lax.dynamic_slice_in_dim(total_sums, first_slot, per_owner, 0)
    owned_tally = lax.dynamic_slice_in_dim(total_tally, first_slot, per_owner, 0)
    sent_unit = unit_rows(gathered).astype(jnp.bfloat16)
    arrived_unit, labels = (
        lax.all_to_all(sent_unit, "docs", split_axis=0, concat_axis=0, tiled=True),
        lax.all_to_all(out_labels, "docs", split_axis=0, concat_axis=0, tiled=True),
    )
    member = label_table(labels, cluster_range)
    centroids = owned_sums / owned_tally[:, None]
    centroid_unit = unit_rows(centroids).astype(jnp.bfloat16)
    lower_table = (slot_range[None, :] < slot_range[:, None]).astype(jnp.float32)
    within = jnp.einsum(
        "ij,njk->nik", lower_table, member, precision=highest, preferred_element_type=jnp.float32
    )
    totals = jnp.sum(member, 1)
    earlier = jnp.cumsum(totals, 0) - totals
    before = jnp.sum((within + earlier[:, None, :]) * member, -1)
    is_live = jnp.sum(member, -1)
    block_range = jnp.arange(block_rows, dtype=jnp.int32).astype(jnp.float32)
    rank_table = (before[:, :, None] == block_range[None, None, :]).astype(jnp.float32) * is_live[
        :, :, None
    ]
    row_number = (
        (jnp.arange(owner_count * capacity, dtype=jnp.int32) + 1)
        .astype(jnp.float32)
        .reshape(owner_count, capacity)
    )
    inverse = jnp.einsum(
        "nck,ncb->kb",
        member * row_number[:, :, None],
        rank_table,
        precision=highest,
        preferred_element_type=jnp.float32,
    ).astype(jnp.int32)
    padded_unit = jnp.concatenate(
        [jnp.zeros((1, feature_width), jnp.bfloat16), arrived_unit.reshape(-1, feature_width)], 0
    )
    blocks = padded_unit[inverse]
    members = jnp.sum(totals, 0)
    gram_blocks = jnp.einsum("kid,kjd->kij", blocks, blocks, preferred_element_type=jnp.float32)
    allowed = (block_range[None, None, :] < members[:, None, None]) & (
        block_range[None, :, None] != block_range[None, None, :]
    )
    nearest = jnp.max(jnp.where(allowed, gram_blocks, -2.0), -1)
    to_centroid = jnp.einsum(
        "kmd,kd->km", blocks, centroid_unit, preferred_element_type=jnp.float32
    )
    nearest_rows = jnp.einsum(
        "nck,kb->ncb", member, nearest, precision=highest, preferred_element_type=jnp.float32
    )
    cosine_rows = jnp.einsum(
        "nck,kb->ncb", member, to_centroid, precision=highest, preferred_element_type=jnp.float32
    )
    nearest_slots = jnp.sum(nearest_rows * rank_table, -1)
    cosine_slots = jnp.sum(cosine_rows * rank_table, -1)
    back_nearest, back_cosine = (
        lax.all_to_all(nearest_slots, "docs", split_axis=0, concat_axis=0, tiled=True),
        lax.all_to_all(cosine_slots, "docs", split_axis=0, concat_axis=0, tiled=True),
    )
    position = jnp.arange(row_count, dtype=jnp.int32) - send_offsets[owner_of_row]
    max_sim = back_nearest[owner_of_row, position]
    centroid_cos = back_cosine[owner_of_row, position]
    return (centroids, max_sim, centroid_cos)


def solution(mesh):
    placed = (P(("grp", "docs"), None), P(("grp", "docs")), P())
    return jax.shard_map(
        per_device,
        mesh=mesh,
        in_specs=placed,
        out_specs=(P("docs", None), P(("grp", "docs")), P(("grp", "docs"))),
        check_vma=False,
    )
```

profile of v0, /device:TPU:0, one launch (start us, length us, event | category | flops | bytes accessed | tf_op | source)
XLA Modules:
  0.0 627.0 jit_solution(15091308752628547597)
XLA Ops:
  7.9 16.7 %gather_fusion = s32[4096]{0:T(1024)S(1)} fusion(s32[768]{0:T(1024)S(1)} %copy-done, s32[4096]{0:T(1024)S(1)} %fusion.57), kind=kCustom, calls=%fused_computation | custom fusion | bytes 49152 | tf_op jit(solution)/shard_map/gather | solution.py:25
  25.1 28.7 %gather_fusion.1 = s32[5120]{0:T(1024)S(1)} fusion(s32[4096]{0:T(1024)S(1)} %get-tuple-element.13, s32[5120]{0:T(1024)S(1)} %broadcast_clamp_fusion), kind=kCustom, calls=%fused_computation.1 | custom fusion | bytes 61440 | tf_op jit(solution)/shard_map/gather | solution.py:34
  54.4 6.3 %all-to-all-start = ((s32[8,1,640]{2,1,0:T(1,128)}), s32[8,1,640]{2,1,0:T(1,128)S(1)}, u32[]{:S(2)}, u32[]{:S(2)}) async-start(s32[8,1,640]{2,1,0:T(1,128)} %compare_select_fusion.3), calls=%async_computation | async-start | bytes 40960 | tf_op jit(solution)/shard_map/all_to_all | solution.py:49
  60.8 33.4 %gather_fusion.2 = f32[5120,1024]{1,0:T(8,128)} fusion(f32[4096,1024]{1,0:T(8,128)} %param.3, s32[5120]{0:T(1024)S(1)} %broadcast_clamp_fusion), kind=kCustom, calls=%fused_computation.2 | custom fusion | bytes 41963520 | tf_op jit(solution)/shard_map/gather | solution.py:36
  94.3 9.0 %multiply_reduce_fusion = f32[8,640]{1,0:T(8,128)S(1)} fusion(f32[8,640,1024]{2,1,0:T(8,128)} %bitcast.70, pred[8,640]{1,0:T(8,128)(4,1)S(1)} %iota_compare_fusion.16), kind=kLoop, calls=%fused_computation.7 | loop fusion | flops 15723520 | bytes 20997120 | tf_op jit(solution)/shard_map/reduce_sum | solution.py:11
  103.3 3.9 copy-done.2
  107.3 5.4 multiply_convert_fusion
  112.7 5.1 all-to-all-start.1
  118.0 14.6 %fusion = f32[8,96,1024]{2,1,0:T(8,128)} fusion(f32[8,640,1024]{2,1,0:T(8,128)} %bitcast.71, pred[8,640]{1,0:T(8,128)(4,1)S(1)} %iota_compare_fusion.16, s32[8,640]{1,0:T(8,128)S(1)} %broadcast_select_fusion), kind=kOutput, calls=%fused_computation.8 | convolution fusion | flops 6045532160 | bytes 24142848 | tf_op jit(solution)/shard_map/nck,ncd->nkd/dot_general | solution.py:38
  133.6 4.4 compare_select_fusion.4
  138.1 267.8 %psum.15 = f32[768]{0:T(1024)S(1)} all-reduce(f32[768]{0:T(1024)S(1)} %reshape.353), channel_id=1, replica_groups=mesh['grp'=4,'docs'=8] {'grp','docs'}, use_global_device_ids=true, to_apply=%region_4.5 | all-reduce | flops 768 | bytes 6144 | tf_op jit(solution)/shard_map/psum | solution.py:42
  407.5 1.0 fusion.9
  408.5 2.8 fusion.51
  411.3 1.2 multiply_reduce_fusion.1
  412.7 10.9 %concatenate.7 = bf16[5121,1024]{1,0:T(8,128)(2,1)} pad(bf16[5120,1024]{1,0:T(8,128)(2,1)} %bitcast.5, bf16[]{:T(256)} %constant.55.clone.1), padding=1_0x0_0 | pad | bytes 20973570 | tf_op jit(solution)/shard_map/concatenate | solution.py:78
  423.6 65.8 %gather_fusion.3 = bf16[12288,1024]{1,0:T(8,128)(2,1)} fusion(bf16[5121,1024]{1,0:T(8,128)(2,1)} %concatenate.7, s32[12288]{0:T(1024)S(1)} %fusion.51), kind=kCustom, calls=%fused_computation.3 | custom fusion | bytes 50380800 | tf_op jit(solution)/shard_map/gather | solution.py:81
  489.4 20.6 %select_reduce_fusion = f32[96,128]{1,0:T(8,128)S(1)} fusion(pred[128,128]{0,1:T(8,128)(4,1)S(1)} %broadcast_compare_fusion, pred[96,128]{1,0:T(8,128)(4,1)S(1)} %broadcast_compare_fusion.1, bf16[96,128,1024]{2,1,0:T(8,128)(2,1)} %bitcast.73), kind=kOutput, calls=%fused_computation.12 | convolution fusion | flops 3225931776 | bytes 25243648 | tf_op jit(solution)/shard_map/kid,kjd->kij/dot_general | solution.py:83
  510.0 1.4 fusion.7
  512.0 3.6 all-to-all-start.2
  515.6 11.5 %fusion.39 = f32[96,1,128]{2,1,0:T(1,128)S(1)} fusion(bf16[96,128,1024]{2,1,0:T(8,128)(2,1)} %bitcast.74, bf16[96,1024,1]{1,0,2:T(8,128)(2,1)S(1)} %fusion.41), kind=kOutput, calls=%fused_computation.47 | convolution fusion | flops 25165824 | bytes 25411584 | tf_op jit(solution)/shard_map/kmd,kd->km/dot_general | solution.py:88
  527.1 1.4 fusion.8
  529.2 5.1 all-to-all-start.3
  534.4 42.9 %gather_fusion.4 = f32[4096]{0:T(1024)} fusion(f32[8,640]{1,0:T(8,128)S(1)} %bitcast.67, s32[4096]{0:T(1024)S(1)} %bitcast.68), kind=kCustom, calls=%fused_computation.4 | custom fusion | bytes 65536 | tf_op jit(solution)/shard_map/gather | solution.py:104
  577.2 42.9 %gather_fusion.5 = f32[4096]{0:T(1024)} fusion(f32[8,640]{1,0:T(8,128)S(1)} %bitcast.66, s32[4096]{0:T(1024)S(1)} %bitcast.69), kind=kCustom, calls=%fused_computation.5 | custom fusion | bytes 65536 | tf_op jit(solution)/shard_map/gather | solution.py:105
  (48 shorter events, 6.1 us)
Async XLA Ops:
  7.2 0.7 copy-start
  54.4 58.2 %all-to-all-start = ((s32[8,1,640]{2,1,0:T(1,128)}), s32[8,1,640]{2,1,0:T(1,128)S(1)}, u32[]{:S(2)}, u32[]{:S(2)}) async-start(s32[8,1,640]{2,1,0:T(1,128)} %compare_select_fusion.3), calls=%async_computation | async-start | bytes 40960 | tf_op jit(solution)/shard_map/all_to_all | solution.py:49
  94.3 13.0 %copy-start.2 = (f32[5120,1024]{1,0:T(8,128)S(1)}, f32[5120,1024]{1,0:T(8,128)}, u32[]{:S(2)}) copy-start(f32[5120,1024]{1,0:T(8,128)} %gather_fusion.2) | copy-start | bytes 62914564
  112.7 300.0 %all-to-all-start.1 = ((bf16[8,640,1024]{2,1,0:T(8,128)(2,1)}), bf16[8,640,1024]{2,1,0:T(8,128)(2,1)}, u32[]{:S(2)}, u32[]{:S(2)}) async-start(bf16[8,640,1024]{2,1,0:T(8,128)(2,1)} %multiply_convert_fusion), calls=%async_computation.1 | async-start | bytes 20971520 | tf_op jit(solution)/shard_map/all_to_all | solution.py:48
  117.8 293.5 %all-reduce.3.cloned.1.call-start = ((), (), s32[]{:S(2)}) async-start(), calls=%async_computation.4 | async-start | bytes 6291456 | tf_op jit(solution)/shard_map/psum | solution.py:42
  412.5 11.1 %copy-start.3 = (f32[96,1024]{1,0:T(8,128)}, f32[96,1024]{1,0:T(8,128)S(1)}, u32[]{:S(2)}) copy-start(f32[96,1024]{1,0:T(8,128)S(1)} %get-tuple-element.7) | copy-start | bytes 1179652
  512.0 17.2 %all-to-all-start.2 = ((f32[8,1,640]{2,1,0:T(1,128)}), f32[8,1,640]{2,1,0:T(1,128)S(1)}, u32[]{:S(2)}, u32[]{:S(2)}) async-start(f32[8,1,640]{2,1,0:T(1,128)} %all_to_all.25), calls=%async_computation.2 | async-start | bytes 40960 | tf_op jit(solution)/shard_map/all_to_all | solution.py:100
  529.2 48.0 %all-to-all-start.3 = ((f32[8,1,640]{2,1,0:T(1,128)}), f32[8,1,640]{2,1,0:T(1,128)S(1)}, u32[]{:S(2)}, u32[]{:S(2)}) async-start(f32[8,1,640]{2,1,0:T(1,128)} %all_to_all.28), calls=%async_computation.3 | async-start | bytes 40960 | tf_op jit(solution)/shard_map/all_to_all | solution.py:101
  577.2 42.9 %copy-start.1 = (s32[768]{0:T(1024)S(1)}, s32[768]{0:T(1024)}, u32[]{:S(2)}) copy-start(s32[768]{0:T(1024)} %param.5) | copy-start | bytes 9220
Sparse Core Ops, SparseCore 0:
  132.7 243.3 all-reduce.2
where the time goes:
time: 628 us; the launch traced here: 627 us
  blocking collectives  268 us (43%)
  local copies, waits for them, and re-layouts  247 us (39%)
  matrix products  53.4 us (9%)
  other arithmetic  24 us (4%)
  starting transfers between devices  20.2 us (3%)
  between operations  14.3 us (2%)
    psum x1, blocking collectives, per_device(): lax.psum((partial_sums, partial_tally), ('grp', 'docs'))  268 us
    gather x1, local copies, waits for them, and re-layouts, per_device(): blocks = padded_unit[inverse]  65.8 us
    gather x1, local copies, waits for them, and re-layouts, per_device(): max_sim = back_nearest[owner_of_row, position]  42.9 us
    gather x1, local copies, waits for them, and re-layouts, per_device(): centroid_cos = back_cosine[owner_of_row, position]  42.9 us
    gather x1, local copies, waits for them, and re-layouts, per_device(): embeddings[source_row]  33.4 us
    gather x2, local copies, waits for them, and re-layouts, per_device(): out_labels = jnp.where(occupied, local_of_row[source_row], per_owner)  28.7 us
    dot_general x1, matrix products, per_device(): jnp.einsum('kid,kjd->kij', blocks, blocks, preferred_element_type=jnp.flo...  20.6 us
    gather x1, local copies, waits for them, and re-layouts, per_device(): slot_of_row = cluster_slot[assign]  16.7 us
  transfers between devices with their start and end apart: 5, of which 0 were waited for; matrix products, arithmetic and copies ran while one was open for 21% of the time, Pallas kernels for 0%

commit v1 on v0

v1 whole, which is shorter than its diff:
```python
import functools

import jax
import jax.numpy as jnp
from jax import lax
from jax.experimental import pallas as pl
from jax.experimental.pallas import tpu as pltpu
from jax.sharding import PartitionSpec as P

epsilon = 1e-06
LANES = 128
SUBLANES = 8
VMEM_BYTES = 48 * 1024 * 1024
in_vmem = pl.BlockSpec(memory_space=pltpu.VMEM)
in_smem = pl.BlockSpec(memory_space=pltpu.SMEM)
anywhere = pl.BlockSpec(memory_space=pl.ANY)


def round_up(value, step):
    return -(-value // step) * step


def params(**extra):
    return pltpu.CompilerParams(vmem_limit_bytes=VMEM_BYTES, **extra)


def look_up(table_ref, index):
    lane = jnp.bitwise_and(index, LANES - 1)
    row = jnp.right_shift(index, 7)
    found = jnp.zeros(index.shape, jnp.int32)
    for part in range(table_ref.shape[0]):
        entries = jnp.broadcast_to(table_ref[part : part + 1, :], index.shape)
        found = jnp.where(row == part, jnp.take_along_axis(entries, lane, axis=1), found)
    return found


def rows_below(slots, bound):
    return jnp.sum((slots < bound).astype(jnp.float32)).astype(jnp.int32)


def plan_kernel(per_owner, limit, assign_ref, table_ref, slot_ref, start_ref):
    slots = look_up(table_ref, assign_ref[...])
    slot_ref[...] = slots
    for owner in range(start_ref.shape[0]):
        start_ref[owner] = jnp.minimum(rows_below(slots, owner * per_owner), limit)


def make_plan(assign_rows, table, owner_count, per_owner, limit):
    return pl.pallas_call(
        functools.partial(plan_kernel, per_owner, limit),
        out_shape=(
            jax.ShapeDtypeStruct(assign_rows.shape, jnp.int32),
            jax.ShapeDtypeStruct((owner_count,), jnp.int32),
        ),
        in_specs=[in_vmem, in_vmem],
        out_specs=(in_vmem, in_smem),
        compiler_params=params(),
        name="plan",
    )(assign_rows, table)


def unit_kernel(steps, start_ref, owner_ref, rows_ref, unit_ref, held, sem):
    capacity = unit_ref.shape[0]
    row_count = rows_ref.shape[0]
    part = capacity // steps
    window = part + SUBLANES
    start = start_ref[owner_ref[0]]

    def first(step):
        begin = start + step * part
        aligned = jnp.minimum(begin // SUBLANES * SUBLANES, row_count - window)
        return pl.multiple_of(aligned, SUBLANES)

    copies = [
        pltpu.make_async_copy(rows_ref.at[pl.ds(first(step), window), :], held.at[step], sem.at[step])
        for step in range(steps)
    ]
    for copy in copies:
        copy.start()
    for step in range(steps):
        copies[step].wait()
        shift = start + step * part - first(step)
        groups = held[step].reshape(window // SUBLANES, SUBLANES, -1)
        turned = pltpu.roll(groups, SUBLANES - shift, 1)
        line = lax.broadcasted_iota(jnp.int32, (part // SUBLANES, SUBLANES, groups.shape[2]), 1)
        values = jnp.where(line < SUBLANES - shift, turned[:-1], turned[1:]).reshape(part, -1)
        scale = lax.rsqrt(jnp.sum(values * values, -1, keepdims=True) + epsilon)
        unit_ref[step * part : (step + 1) * part, :] = (values * scale).astype(jnp.bfloat16)


def unit_chunk(starts, owner, embeddings, capacity):
    width = embeddings.shape[1]
    steps = 5 if capacity % 80 == 0 and capacity >= 320 else 1
    part = capacity // steps
    return pl.pallas_call(
        functools.partial(unit_kernel, steps),
        out_shape=jax.ShapeDtypeStruct((capacity, width), jnp.bfloat16),
        in_specs=[in_smem, in_smem, anywhere],
        out_specs=in_vmem,
        scratch_shapes=[
            pltpu.VMEM((steps, part + SUBLANES, width), jnp.float32),
            pltpu.SemaphoreType.DMA((steps,)),
        ],
        compiler_params=params(),
        cost_estimate=pl.CostEstimate(
            flops=4 * capacity * width, bytes_accessed=6 * capacity * width, transcendentals=capacity
        ),
        name="unit",
    )(starts, owner, embeddings)


def aligned_start(start, row_count, window):
    begin = jnp.minimum(jnp.left_shift(jnp.right_shift(start, 3), 3), row_count - window)
    return pl.multiple_of(begin, SUBLANES)


def flat_window(held, start, rows):
    span = round_up(rows + 1, SUBLANES)
    shift = jnp.bitwise_and(start, LANES - 1)
    block = held[pl.ds(jnp.right_shift(start, 7), span), :]
    turned = pltpu.roll(block, jnp.bitwise_and(LANES - shift, LANES - 1), 1)
    following = pltpu.roll(turned, span - 1, 0)
    lane = lax.broadcasted_iota(jnp.int32, block.shape, 1)
    return jnp.where(lane < LANES - shift, turned, following)


def window_labels(held, slots, owner, start, per_owner, capacity, blocks):
    low = owner * per_owner
    mine = (slots >= low) & (slots < low + per_owner)
    held[: slots.shape[0], :] = jnp.where(mine, slots - low, -1)
    labels = flat_window(held, start, blocks)
    place = lax.broadcasted_iota(jnp.int32, labels.shape, 0) * LANES + lax.broadcasted_iota(
        jnp.int32, labels.shape, 1
    )
    return jnp.where(place < capacity, labels, -1)


def label_kernel(
    per_owner, limit, capacity, order_ref, me_ref, start_ref, slot_ref, group_ref, table_ref,
    sent_ref, row_ref, column_ref, tally_ref, held,
):
    source_count, padded = row_ref.shape
    blocks = padded // LANES
    held[...] = jnp.full(held.shape, -1, jnp.int32)
    slots = slot_ref[...]
    window = capacity + SUBLANES
    for owner in range(source_count):
        start = aligned_start(start_ref[owner], slots.size, window)
        wide = sent_ref.shape[1] // LANES
        labels = window_labels(held, slots, owner, start, per_owner, window, wide)
        for block in range(wide):
            sent_ref[owner : owner + 1, block * LANES : (block + 1) * LANES] = labels[block : block + 1, :]
    me = me_ref[0]
    tally = jnp.zeros(tally_ref.shape, jnp.float32)
    cluster = lax.broadcasted_iota(jnp.int32, tally.shape, 0)
    for place in range(source_count):
        slots = look_up(table_ref, group_ref[order_ref[place]])
        start = jnp.minimum(rows_below(slots, me * per_owner), limit)
        labels = window_labels(held, slots, me, start, per_owner, capacity, blocks)
        for block in range(blocks):
            row = labels[block : block + 1, :]
            spread = jnp.broadcast_to(row, (LANES, LANES))
            row_ref[place : place + 1, block * LANES : (block + 1) * LANES] = row
            column_ref[place, block * LANES : (block + 1) * LANES, :] = spread.T
            tally += (jnp.broadcast_to(row, tally.shape) == cluster).astype(jnp.float32)
    tally_ref[...] = jnp.broadcast_to(jnp.sum(tally, 1, keepdims=True), tally_ref.shape)


def make_labels(order, me, starts, slots, group_assign, table, per_owner, limit, capacity, padded):
    source_count = group_assign.shape[0]
    return pl.pallas_call(
        functools.partial(label_kernel, per_owner, limit, capacity),
        out_shape=(
            jax.ShapeDtypeStruct((source_count, round_up(capacity + SUBLANES, LANES)), jnp.int32),
            jax.ShapeDtypeStruct((source_count, padded), jnp.int32),
            jax.ShapeDtypeStruct((source_count, padded, LANES), jnp.int32),
            jax.ShapeDtypeStruct((per_owner, LANES), jnp.float32),
        ),
        in_specs=[in_smem, in_smem, in_smem, in_vmem, in_vmem, in_vmem],
        out_specs=(in_vmem, in_vmem, in_vmem, in_vmem),
        scratch_shapes=[pltpu.VMEM((slots.shape[0] + 2 * SUBLANES, LANES), jnp.int32)],
        compiler_params=params(),
        name="labels",
    )(order, me, starts, slots, group_assign, table)


def sum_kernel(start_ref, label_ref, rows_ref, sum_ref, held, sem):
    owner_count, per_owner, _ = sum_ref.shape
    window = held.shape[1]

    def copy(owner, slot):
        first = aligned_start(start_ref[owner], rows_ref.shape[0], window)
        return pltpu.make_async_copy(rows_ref.at[pl.ds(first, window), :], held.at[slot], sem.at[slot])

    copy(0, 0).start()

    def body(owner, carry):
        slot = lax.rem(owner, 2)

        @pl.when(owner + 1 < owner_count)
        def _():
            copy(owner + 1, 1 - slot).start()

        copy(owner, slot).wait()
        labels = label_ref[pl.ds(owner, 1), :][:, :window]
        cluster = lax.broadcasted_iota(jnp.int32, (per_owner, window), 0)
        member = (labels == cluster).astype(jnp.float32).astype(jnp.bfloat16)
        values = held[slot]
        high = values.astype(jnp.bfloat16)
        rest = values - high.astype(jnp.float32)
        middle = rest.astype(jnp.bfloat16)
        low = (rest - middle.astype(jnp.float32)).astype(jnp.bfloat16)
        total = jnp.dot(member, high, preferred_element_type=jnp.float32)
        total += jnp.dot(member, middle, preferred_element_type=jnp.float32)
        total += jnp.dot(member, low, preferred_element_type=jnp.float32)
        sum_ref[pl.ds(owner, 1)] = total[None]
        return carry

    lax.fori_loop(0, owner_count, body, 0)


def slot_sums(starts, sent_labels, embeddings, per_owner, capacity):
    owner_count = sent_labels.shape[0]
    width = embeddings.shape[1]
    return pl.pallas_call(
        sum_kernel,
        out_shape=jax.ShapeDtypeStruct((owner_count, per_owner, width), jnp.float32),
        in_specs=[in_smem, in_vmem, anywhere],
        out_specs=in_vmem,
        scratch_shapes=[
            pltpu.VMEM((2, capacity + SUBLANES, width), jnp.float32),
            pltpu.SemaphoreType.DMA((2,)),
        ],
        compiler_params=params(),
        cost_estimate=pl.CostEstimate(
            flops=6 * owner_count * per_owner * capacity * width,
            bytes_accessed=4 * embeddings.size,
            transcendentals=0,
        ),
        name="sums",
    )(starts, sent_labels, embeddings)


def gram_kernel(count, capacity, row_ref, column_ref, best_ref, *refs):
    chunks, out_ref, held, best, sem = refs[:count], *refs[count:]
    padded = held.shape[1]
    last = count - 1
    copies = [
        pltpu.make_async_copy(chunks[place], held.at[place, pl.ds(0, capacity), :], sem.at[place])
        for place in range(count)
    ]
    for place in (last, *range(last)):
        copies[place].start()
    if capacity < padded:
        for place in range(count):
            held[place, capacity:, :] = jnp.zeros((padded - capacity, held.shape[2]), held.dtype)
    out_ref[...] = best_ref[...]
    labels = column_ref[0]
    spread = jnp.concatenate([labels] * (padded // LANES), 1)

    def similarity(place):
        return lax.dot_general(
            held[last], held[place], (((1,), (1,)), ((), ())), preferred_element_type=jnp.float32
        )

    copies[last].wait()
    row = lax.broadcasted_iota(jnp.int32, (padded, padded), 0)
    column = lax.broadcasted_iota(jnp.int32, (padded, padded), 1)
    allowed = (spread == row_ref[last : last + 1, :]) & (row != column)
    nearest = jnp.max(jnp.where(allowed, similarity(last), -2.0), 0, keepdims=True)
    best[...] = jnp.full(best.shape, -2.0, jnp.float32)
    for place in range(last):
        copies[place].wait()

    def body(place, carry):
        near = jnp.where(spread == row_ref[pl.ds(place, 1), :], similarity(place), -2.0)
        out_ref[pl.ds(place, 1), :] = jnp.maximum(
            out_ref[pl.ds(place, 1), :], jnp.max(near, 0, keepdims=True)
        )
        folded = best[...]
        for block in range(padded // LANES):
            folded = jnp.maximum(folded, near[:, block * LANES : (block + 1) * LANES])
        best[...] = folded
        return carry

    if last:
        lax.fori_loop(0, last, body, 0)
        for block in range(padded // LANES):
            part = slice(block * LANES, (block + 1) * LANES)
            other = jnp.max(best[part, :].T, 0, keepdims=True)
            out_ref[last : last + 1, part] = jnp.maximum(nearest[:, part], other)
    else:
        out_ref[last : last + 1, :] = nearest


def gram_step(rows, columns, best, chunks, capacity):
    count = len(chunks)
    padded = rows.shape[1]
    width = chunks[0].shape[1]
    last = count - 1
    return pl.pallas_call(
        functools.partial(gram_kernel, count, capacity),
        out_shape=jax.ShapeDtypeStruct(best.shape, jnp.float32),
        grid=(1,),
        in_specs=[
            pl.BlockSpec(rows.shape, lambda step: (0, 0)),
            pl.BlockSpec((1, padded, LANES), lambda step: (last, 0, 0)),
            pl.BlockSpec(best.shape, lambda step: (0, 0)),
        ]
        + [anywhere] * count,
        out_specs=pl.BlockSpec(best.shape, lambda step: (0, 0)),
        scratch_shapes=[
            pltpu.VMEM((count, padded, width), jnp.bfloat16),
            pltpu.VMEM((padded, LANES), jnp.float32),
            pltpu.SemaphoreType.DMA((count,)),
        ],
        compiler_params=params(),
        cost_estimate=pl.CostEstimate(
            flops=2 * count * padded * padded * width,
            bytes_accessed=2 * count * capacity * width,
            transcendentals=0,
        ),
        name="gram",
    )(rows, columns, best, *chunks)


def centroid_kernel(sum_ref, tally_ref, centroid_ref, unit_ref):
    tally = jnp.concatenate([tally_ref[...]] * (sum_ref.shape[1] // LANES), 1)
    centroids = sum_ref[...] / tally
    centroid_ref[...] = centroids
    scale = lax.rsqrt(jnp.sum(centroids * centroids, -1, keepdims=True) + epsilon)
    unit_ref[...] = (centroids * scale).astype(jnp.bfloat16)


def make_centroids(sums, tally):
    return pl.pallas_call(
        centroid_kernel,
        out_shape=(
            jax.ShapeDtypeStruct(sums.shape, jnp.float32),
            jax.ShapeDtypeStruct(sums.shape, jnp.bfloat16),
        ),
        in_specs=[in_vmem, in_vmem],
        out_specs=(in_vmem, in_vmem),
        compiler_params=params(),
        name="centroids",
    )(sums, tally)


def cosine_kernel(order_ref, row_ref, best_ref, centroid_ref, *refs):
    count = row_ref.shape[0]
    chunks, out_ref = refs[:count], refs[count]
    capacity = chunks[0].shape[0]
    for place in range(count):
        products = lax.dot_general(
            centroid_ref[...], chunks[place][...], (((1,), (1,)), ((), ())), preferred_element_type=jnp.float32
        )
        cluster = lax.broadcasted_iota(jnp.int32, products.shape, 0)
        mine = row_ref[place : place + 1, :][:, :capacity] == cluster
        cosine = jnp.sum(jnp.where(mine, products, 0.0), 0, keepdims=True)
        source = order_ref[place]
        out_ref[source, 0:1, :] = best_ref[place : place + 1, :]
        if capacity < row_ref.shape[1]:
            out_ref[source, 1:2, :] = jnp.zeros((1, row_ref.shape[1]), jnp.float32)
        out_ref[source, 1:2, :capacity] = cosine


def make_cosines(order, rows, best, centroid_unit, chunks):
    count, padded = rows.shape
    return pl.pallas_call(
        cosine_kernel,
        out_shape=jax.ShapeDtypeStruct((count, 2, padded), jnp.float32),
        in_specs=[in_smem] + [in_vmem] * (3 + count),
        out_specs=in_vmem,
        compiler_params=params(),
        name="cosines",
    )(order, rows, best, centroid_unit, *chunks)


def place_kernel(per_owner, start_ref, slot_ref, back_ref, near_ref, cosine_ref, held, lines, result):
    owner_count, _, padded = back_ref.shape
    blocks = padded // LANES
    rows = slot_ref.shape[0]
    span = round_up(blocks + 1, SUBLANES)
    held[...] = jnp.full(held.shape, -1, jnp.int32)
    held[:rows, :] = slot_ref[...]
    result[...] = jnp.zeros(result.shape, jnp.float32)
    lines[...] = jnp.zeros(lines.shape, jnp.float32)
    lane = lax.broadcasted_iota(jnp.int32, (span, LANES), 1)
    for owner in range(owner_count):
        start = start_ref[owner]
        first = pl.ds(jnp.right_shift(start, 7), span)
        shift = jnp.bitwise_and(start, LANES - 1)
        slots = held[first, :]
        mine = (slots >= owner * per_owner) & (slots < (owner + 1) * per_owner)
        for kind in range(2):
            for block in range(blocks):
                lines[block : block + 1, :] = back_ref[owner, kind : kind + 1, block * LANES : (block + 1) * LANES]
            turned = pltpu.roll(lines[...], shift, 1)
            earlier = pltpu.roll(turned, 1, 0)
            moved = jnp.where(lane >= shift, turned, earlier)
            result[kind, first, :] = jnp.where(mine, moved, result[kind, first, :])
    near_ref[...] = result[0, :rows, :]
    cosine_ref[...] = result[1, :rows, :]


def place_rows(starts, slots, back, per_owner):
    padded = back.shape[2]
    span = round_up(padded // LANES + 1, SUBLANES)
    rows = slots.shape[0]
    return pl.pallas_call(
        functools.partial(place_kernel, per_owner),
        out_shape=(jax.ShapeDtypeStruct(slots.shape, jnp.float32),) * 2,
        in_specs=[in_smem, in_vmem, in_vmem],
        out_specs=(in_vmem, in_vmem),
        scratch_shapes=[
            pltpu.VMEM((rows + span, LANES), jnp.int32),
            pltpu.VMEM((span, LANES), jnp.float32),
            pltpu.VMEM((2, rows + span, LANES), jnp.float32),
        ],
        compiler_params=params(),
        name="place",
    )(starts, slots, back)


def turns(count):
    return sorted(range(count), key=lambda turn: (turn != 0, abs(turn - count // 2), turn))


def per_device(embeddings, assign, cluster_slot):
    row_count, width = embeddings.shape
    owner_count = lax.axis_size("docs")
    group_count = lax.axis_size("grp")
    per_owner = cluster_slot.shape[0] // owner_count
    capacity = row_count // owner_count + row_count // (4 * owner_count)
    padded = round_up(capacity, LANES)
    limit = row_count - capacity
    me = lax.axis_index("docs").astype(jnp.int32)
    order_of = turns(owner_count)

    assign_rows = assign.reshape(-1, LANES)
    table = cluster_slot.reshape(-1, LANES)
    group_assign = lax.all_gather(assign_rows, "docs")
    slots, starts = make_plan(assign_rows, table, owner_count, per_owner, limit)

    chunks = {}
    for turn in order_of[1:] + order_of[:1]:
        owner = lax.rem(me + turn, owner_count).reshape(1)
        chunk = unit_chunk(starts, owner, embeddings, capacity)
        if turn:
            pairs = [(i, (i + turn) % owner_count) for i in range(owner_count)]
            chunk = lax.ppermute(chunk, "docs", pairs)
        chunks[turn] = chunk
    arrived = [chunks[turn] for turn in order_of]
    order = jnp.stack([lax.rem(me + owner_count - turn, owner_count) for turn in order_of])

    sent_labels, rows, columns, group_tally = make_labels(
        order, me.reshape(1), starts, slots, group_assign, table, per_owner, limit, capacity, padded
    )
    partial_sums = slot_sums(starts, sent_labels, embeddings, per_owner, capacity)
    share = lax.psum_scatter(partial_sums, "grp", scatter_dimension=1, tiled=True)
    share = lax.psum_scatter(share, "docs", scatter_dimension=0, tiled=True)[0]
    sums = lax.all_gather(share, "grp", axis=0, tiled=True)
    tally = lax.psum(group_tally, "grp")
    centroids, centroid_unit = make_centroids(sums, tally)

    best = jnp.full((owner_count, padded), -2.0, jnp.float32)
    for count in range(1, owner_count + 1):
        best = gram_step(rows, columns, best, arrived[:count], capacity)
    results = make_cosines(order, rows, best, centroid_unit, arrived)
    back = lax.all_to_all(results, "docs", split_axis=0, concat_axis=0, tiled=True)
    near, cosine = place_rows(starts, slots, back, per_owner)
    return (centroids, near.reshape(-1), cosine.reshape(-1))


def solution(mesh):
    placed = (P(("grp", "docs"), None), P(("grp", "docs")), P())
    return jax.shard_map(
        per_device,
        mesh=mesh,
        in_specs=placed,
        out_specs=(P("docs", None), P(("grp", "docs")), P(("grp", "docs"))),
        check_vma=False,
    )
```

time: 628 us -> 357 us (0.57)
  local copies, waits for them, and re-layouts: 247 us -> 5.42 us
  blocking collectives: 268 us -> 56.9 us
  waiting for transfers between devices: 0.05 us -> 153 us
  Pallas kernels: 0 us -> 119 us
  matrix products: 53.4 us -> 0 us
  other arithmetic: 24 us -> 0 us
  starting transfers between devices: 20.2 us -> 8.04 us
    psum x1, blocking collectives: 268 us -> 17.5 us  [per_device(): tally = lax.psum(group_tally, 'grp')]
    gather x8 -> x0, local copies, waits for them, and re-layouts: 231 us -> none  [the longest x1 65.8 us: per_device(): blocks = padded_unit[inverse]]
    pallas_call x0 -> x22, Pallas kernels: none -> 119 us  [the longest x8 63.9 us: gram_step(): pl.pallas_call(functools.partial(gram_kernel, count, capacity), out_shape...]
    ppermute x0 -> x7, waiting for transfers between devices: none -> 116 us  [per_device(): chunk = lax.ppermute(chunk, 'docs', pairs)]
    dot_general x7 -> x0, matrix products: 53.4 us -> none  [the longest x1 20.6 us: per_device(): jnp.einsum('kid,kjd->kij', blocks, blocks, preferred_element_type=jnp.flo...]
    reduce_scatter x0 -> x2, waiting for transfers between devices: none -> 37.3 us  [the longest x1 37.2 us: per_device(): share = lax.psum_scatter(share, 'docs', scatter_dimension=0, tiled=True)[0]]
    all_gather x0 -> x2, blocking collectives: none -> 26 us  [the longest x1 15.9 us: per_device(): group_assign = lax.all_gather(assign_rows, 'docs')]
    all_to_all x4 -> x0, starting transfers between devices: 20.1 us -> none  [the longest x1 6.33 us: per_device(): lax.all_to_all(out_labels, 'docs', split_axis=0, concat_axis=0, tiled=True)]
  transfers between devices with their start and end apart: 5 -> 9, of which waited for: 0 -> 3; matrix products, arithmetic and copies ran while one was open for 21% -> 0% of each run, Pallas kernels for 0% -> 25%
where the time goes in v1:
time: 357 us; the launch traced here: 356 us
  waiting for transfers between devices  153 us (43%)
  Pallas kernels  119 us (33%)
  blocking collectives  56.9 us (16%)
  between operations  14.3 us (4%)
  starting transfers between devices  8.04 us (2%)
  local copies, waits for them, and re-layouts  5.42 us (2%)
    ppermute x7, waiting for transfers between devices, per_device(): chunk = lax.ppermute(chunk, 'docs', pairs)  116 us
    pallas_call x8, Pallas kernels, gram_step(): pl.pallas_call(functools.partial(gram_kernel, count, capacity), out_shape...  63.9 us
    reduce_scatter x1, waiting for transfers between devices, per_device(): share = lax.psum_scatter(share, 'docs', scatter_dimension=0, tiled=True)[0]  37.2 us
    pallas_call x8, Pallas kernels, unit_chunk(): pl.pallas_call(functools.partial(unit_kernel, steps), out_shape=jax.Shape...  26.9 us
    psum x1, blocking collectives, per_device(): tally = lax.psum(group_tally, 'grp')  17.5 us
    all_gather x1, blocking collectives, per_device(): group_assign = lax.all_gather(assign_rows, 'docs')  15.9 us
    pallas_call x1, Pallas kernels, slot_sums(): pl.pallas_call(sum_kernel, out_shape=jax.ShapeDtypeStruct((owner_count, p...  14.9 us
    all_to_all x1, blocking collectives, per_device(): lax.all_to_all(results, 'docs', split_axis=0, concat_axis=0, tiled=True)  13.3 us
  transfers between devices with their start and end apart: 9, of which 3 were waited for; matrix products, arithmetic and copies ran while one was open for 0% of the time, Pallas kernels for 25%

profile of v1, /device:TPU:0, one launch (start us, length us, event | category | flops | bytes accessed | tf_op | source)
XLA Modules:
  0.0 356.4 jit_solution(804967274244189362)
XLA Ops:
  7.2 15.9 %all_gather.6.group_ref = s32[8,32,128]{2,1,0:T(8,128)S(1)} all-gather(s32[1,32,128]{2,1,0:T(8,128)} %bitcast.17), channel_id=1, replica_groups=mesh['grp'=4,'docs'=8] {'docs'}, dimensions={0}, use_global_device_ids=true | all-gather | bytes 147456 | tf_op jit(solution)/shard_map/all_gather | solution.py:442
  30.8 14.9 %sums.1 = f32[8,96,1024]{2,1,0:T(8,128)} custom-call(s32[8]{0:T(128)S(1)} %get-tuple-element.13.start_ref, s32[8,768]{1,0:T(8,128)S(1)} %get-tuple-element.15.label_ref, f32[4096,1024]{1,0:T(8,128)} %rows_ref.17), custom_call_target="tpu_custom_call" | custom-call | flops 3019898880 | bytes 16777216 | tf_op jit(solution)/shard_map/sums/pallas_call | solution.py:225
  45.8 3.6 %unit.9 = bf16[640,1024]{1,0:T(8,128)(2,1)} custom-call(s32[8]{0:T(128)S(1)} %get-tuple-element.13.start_ref, s32[1]{0:T(128)} %bitcast.3.owner_ref, f32[4096,1024]{1,0:T(8,128)} %rows_ref.17), custom_call_target="tpu_custom_call" | custom-call | flops 2621440 | bytes 3932160 | tf_op jit(solution)/shard_map/unit/pallas_call | solution.py:95
  50.1 3.5 unit.10
  53.6 3.3 collective-permute-start.1
  56.9 3.6 %unit.11 = bf16[640,1024]{1,0:T(8,128)(2,1)} custom-call(s32[8]{0:T(128)S(1)} %get-tuple-element.13.start_ref, s32[1]{0:T(128)} %bitcast.4.owner_ref, f32[4096,1024]{1,0:T(8,128)} %rows_ref.17), custom_call_target="tpu_custom_call" | custom-call | flops 2621440 | bytes 3932160 | tf_op jit(solution)/shard_map/unit/pallas_call | solution.py:95
  60.6 3.6 %unit.12 = bf16[640,1024]{1,0:T(8,128)(2,1)} custom-call(s32[8]{0:T(128)S(1)} %get-tuple-element.13.start_ref, s32[1]{0:T(128)} %bitcast.7.owner_ref, f32[4096,1024]{1,0:T(8,128)} %rows_ref.17), custom_call_target="tpu_custom_call" | custom-call | flops 2621440 | bytes 3932160 | tf_op jit(solution)/shard_map/unit/pallas_call | solution.py:95
  64.2 3.3 collective-permute-start.3
  70.6 3.6 %unit.15 = bf16[640,1024]{1,0:T(8,128)(2,1)} custom-call(s32[8]{0:T(128)S(1)} %get-tuple-element.13.start_ref, s32[1]{0:T(128)} %bitcast.8.owner_ref, f32[4096,1024]{1,0:T(8,128)} %rows_ref.17), custom_call_target="tpu_custom_call" | custom-call | flops 2621440 | bytes 3932160 | tf_op jit(solution)/shard_map/unit/pallas_call | solution.py:95
  74.3 3.6 unit.14
  80.7 17.5 %psum.7.tally_ref = f32[96,128]{1,0:T(8,128)S(1)} all-reduce(f32[96,128]{1,0:T(8,128)S(1)} %get-tuple-element.16), channel_id=1, replica_groups=mesh['grp'=4,'docs'=8] {'grp'}, use_global_device_ids=true, to_apply=%region_2.0 | all-reduce | flops 12288 | bytes 98304 | tf_op jit(solution)/shard_map/psum | solution.py:463
  101.3 79.3 %collective-permute-done.refs_1_ = bf16[640,1024]{1,0:T(8,128)(2,1)} collective-permute-done((bf16[640,1024]{1,0:T(8,128)(2,1)}, bf16[640,1024]{1,0:T(8,128)(2,1)}, u32[]{:S(2)}, u32[]{:S(2)}) %collective-permute-start) | collective-permute-done | bytes 1310752 | tf_op jit(solution)/shard_map/ppermute | solution.py:451
  180.7 4.5 %gram.9.best_ref = f32[8,640]{1,0:T(8,128)S(1)} custom-call(s32[8,640]{1,0:T(8,128)S(1)} %get-tuple-element.18.row_ref, s32[8,640,128]{2,1,0:T(8,128)S(1)} %copy-done.1, f32[8,640]{1,0:T(8,128)S(1)} %gram.8.best_ref, bf16[640,1024]{1,0:T(8,128)(2,1)S(1)} %unit.8.refs_0_, bf16[640,1024]{1,0:T(8,128)(2,1)} %collective-permute-done.refs_1_), custom_call_target="tpu_custom_call" | custom-call | flops 1677721600 | bytes 2621440 | tf_op jit(solution)/shard_map/gram/pallas_call | solution.py:301
  185.2 36.5 %collective-permute-done.1.refs_2_ = bf16[640,1024]{1,0:T(8,128)(2,1)} collective-permute-done((bf16[640,1024]{1,0:T(8,128)(2,1)}, bf16[640,1024]{1,0:T(8,128)(2,1)}, u32[]{:S(2)}, u32[]{:S(2)}) %collective-permute-start.1) | collective-permute-done | bytes 1310752 | tf_op jit(solution)/shard_map/ppermute | solution.py:451
  221.7 6.2 %gram.10.best_ref = f32[8,640]{1,0:T(8,128)S(1)} custom-call(s32[8,640]{1,0:T(8,128)S(1)} %get-tuple-element.18.row_ref, s32[8,640,128]{2,1,0:T(8,128)} %copy-done, f32[8,640]{1,0:T(8,128)S(1)} %gram.9.best_ref, bf16[640,1024]{1,0:T(8,128)(2,1)S(1)} %unit.8.refs_0_, bf16[640,1024]{1,0:T(8,128)(2,1)} %collective-permute-done.refs_1_, ...), custom_call_target="tpu_custom_call" | custom-call | flops 2516582400 | bytes 3932160 | tf_op jit(solution)/shard_map/gram/pallas_call | solution.py:301
  227.9 7.4 %gram.11.best_ref = f32[8,640]{1,0:T(8,128)S(1)} custom-call(s32[8,640]{1,0:T(8,128)S(1)} %get-tuple-element.18.row_ref, s32[8,640,128]{2,1,0:T(8,128)} %copy-done, f32[8,640]{1,0:T(8,128)S(1)} %gram.10.best_ref, bf16[640,1024]{1,0:T(8,128)(2,1)S(1)} %unit.8.refs_0_, bf16[640,1024]{1,0:T(8,128)(2,1)} %collective-permute-done.refs_1_, ...), custom_call_target="tpu_custom_call" | custom-call | flops 3355443200 | bytes 5242880 | tf_op jit(solution)/shard_map/gram/pallas_call | solution.py:301
  235.3 8.7 %gram.12.best_ref = f32[8,640]{1,0:T(8,128)S(1)} custom-call(s32[8,640]{1,0:T(8,128)S(1)} %get-tuple-element.18.row_ref, s32[8,640,128]{2,1,0:T(8,128)} %copy-done, f32[8,640]{1,0:T(8,128)S(1)} %gram.11.best_ref, bf16[640,1024]{1,0:T(8,128)(2,1)S(1)} %unit.8.refs_0_, bf16[640,1024]{1,0:T(8,128)(2,1)} %collective-permute-done.refs_1_, ...), custom_call_target="tpu_custom_call" | custom-call | flops 4194304000 | bytes 6553600 | tf_op jit(solution)/shard_map/gram/pallas_call | solution.py:301
  244.1 10.3 %gram.13.best_ref = f32[8,640]{1,0:T(8,128)S(1)} custom-call(s32[8,640]{1,0:T(8,128)S(1)} %get-tuple-element.18.row_ref, s32[8,640,128]{2,1,0:T(8,128)} %copy-done, f32[8,640]{1,0:T(8,128)S(1)} %gram.12.best_ref, bf16[640,1024]{1,0:T(8,128)(2,1)S(1)} %unit.8.refs_0_, bf16[640,1024]{1,0:T(8,128)(2,1)} %collective-permute-done.refs_1_, ...), custom_call_target="tpu_custom_call" | custom-call | flops 5033164800 | bytes 7864320 | tf_op jit(solution)/shard_map/gram/pallas_call | solution.py:301
  254.4 11.9 %gram.14.best_ref = f32[8,640]{1,0:T(8,128)S(1)} custom-call(s32[8,640]{1,0:T(8,128)S(1)} %get-tuple-element.18.row_ref, s32[8,640,128]{2,1,0:T(8,128)} %copy-done, f32[8,640]{1,0:T(8,128)S(1)} %gram.13.best_ref, bf16[640,1024]{1,0:T(8,128)(2,1)S(1)} %unit.8.refs_0_, bf16[640,1024]{1,0:T(8,128)(2,1)} %collective-permute-done.refs_1_, ...), custom_call_target="tpu_custom_call" | custom-call | flops 5872025600 | bytes 9175040 | tf_op jit(solution)/shard_map/gram/pallas_call | solution.py:301
  266.3 13.5 %gram.15.best_ref = f32[8,640]{1,0:T(8,128)S(1)} custom-call(s32[8,640]{1,0:T(8,128)S(1)} %get-tuple-element.18.row_ref, s32[8,640,128]{2,1,0:T(8,128)} %copy-done, f32[8,640]{1,0:T(8,128)S(1)} %gram.14.best_ref, bf16[640,1024]{1,0:T(8,128)(2,1)S(1)} %unit.8.refs_0_, bf16[640,1024]{1,0:T(8,128)(2,1)} %collective-permute-done.refs_1_, ...), custom_call_target="tpu_custom_call" | custom-call | flops 6710886400 | bytes 10485760 | tf_op jit(solution)/shard_map/gram/pallas_call | solution.py:301
  279.8 37.2 %reduce-scatter.5.cloned.1.call-done = f32[1,24,1024]{2,1,0:T(8,128)} async-done(((f32[8,24,1024]{2,1,0:T(8,128)}), f32[1,24,1024]{2,1,0:T(8,128)}) %reduce-scatter.5.cloned.1.call-update) | async-done | bytes 98320 | tf_op jit(solution)/shard_map/reduce_scatter | solution.py:461
  317.1 10.1 %all-gather = f32[1,96,1024]{2,1,0:T(8,128)S(1)} all-gather(f32[1,24,1024]{2,1,0:T(8,128)} %reduce-scatter.5.cloned.1.call-done), channel_id=2, replica_groups=mesh['grp'=4,'docs'=8] {'grp'}, dimensions={1}, use_global_device_ids=true | all-gather | bytes 491520 | tf_op jit(solution)/shard_map/all_gather | solution.py:462
  328.0 6.9 %cosines.1 = f32[8,2,640]{2,1,0:T(2,128)S(1)} custom-call(s32[8]{0:T(128)S(1)} %stack.35.order_ref, s32[8,640]{1,0:T(8,128)S(1)} %get-tuple-element.18.row_ref, f32[8,640]{1,0:T(8,128)S(1)} %gram.15.best_ref, bf16[96,1024]{1,0:T(8,128)(2,1)S(1)} %get-tuple-element.20.centroid_ref, bf16[640,1024]{1,0:T(8,128)(2,1)S(1)} %unit.8.refs_0_, ...), custom_call_target="tpu_custom_call" | custom-call | tf_op jit(solution)/shard_map/cosines/pallas_call | solution.py:369
  334.9 13.3 %all_to_all.5.back_ref = f32[8,2,640]{2,1,0:T(2,128)S(1)} all-to-all(f32[8,2,640]{2,1,0:T(2,128)S(1)} %cosines.1), channel_id=1, replica_groups=mesh['grp'=4,'docs'=8] {'docs'}, dimensions={0} | all-to-all | bytes 81920 | tf_op jit(solution)/shard_map/all_to_all | solution.py:470
  (34 shorter events, 19.7 us)
Async XLA Ops:
  7.2 236.9 %reduce-scatter.3.cloned.1.call-start = ((), (), s32[]{:S(2)}) async-start(), calls=%async_computation.3 | async-start | bytes 3932160 | tf_op jit(solution)/shard_map/reduce_scatter | solution.py:460
  23.1 0.7 copy-start.2
  23.9 0.7 copy-start.3
  25.5 0.7 copy-start.4
  29.3 1.5 copy-start
  45.7 271.3 %reduce-scatter.5.cloned.1.call-start = ((), (), s32[]{:S(2)}) async-start(), calls=%async_computation.4 | async-start | bytes 884736 | tf_op jit(solution)/shard_map/reduce_scatter | solution.py:461
  49.4 131.2 %collective-permute-start = (bf16[640,1024]{1,0:T(8,128)(2,1)}, bf16[640,1024]{1,0:T(8,128)(2,1)}, u32[]{:S(2)}, u32[]{:S(2)}) collective-permute-start(bf16[640,1024]{1,0:T(8,128)(2,1)} %unit.9), channel_id=1, source_target_pairs={{0,4},{1,5},{2,6},{3,7},{4,0},{5,1},{6,2},{7,3},{8,12},{9,13},{10,... | collective-permute-start | bytes 3932168 | tf_op jit(solution)/shard_map/ppermute | solution.py:451
  53.6 168.0 %collective-permute-start.1 = (bf16[640,1024]{1,0:T(8,128)(2,1)}, bf16[640,1024]{1,0:T(8,128)(2,1)}, u32[]{:S(2)}, u32[]{:S(2)}) collective-permute-start(bf16[640,1024]{1,0:T(8,128)(2,1)} %unit.10), channel_id=1, source_target_pairs={{0,3},{1,4},{2,5},{3,6},{4,7},{5,0},{6,1},{7,2},{8,11},{9,12},{10,... | collective-permute-start | bytes 3932168 | tf_op jit(solution)/shard_map/ppermute | solution.py:451
  60.5 167.3 %collective-permute-start.2 = (bf16[640,1024]{1,0:T(8,128)(2,1)}, bf16[640,1024]{1,0:T(8,128)(2,1)}, u32[]{:S(2)}, u32[]{:S(2)}) collective-permute-start(bf16[640,1024]{1,0:T(8,128)(2,1)} %unit.11), channel_id=1, source_target_pairs={{0,5},{1,6},{2,7},{3,0},{4,1},{5,2},{6,3},{7,4},{8,13},{9,14},{10,... | collective-permute-start | bytes 3932168 | tf_op jit(solution)/shard_map/ppermute | solution.py:451
  64.2 171.2 %collective-permute-start.3 = (bf16[640,1024]{1,0:T(8,128)(2,1)}, bf16[640,1024]{1,0:T(8,128)(2,1)}, u32[]{:S(2)}, u32[]{:S(2)}) collective-permute-start(bf16[640,1024]{1,0:T(8,128)(2,1)} %unit.12), channel_id=1, source_target_pairs={{0,2},{1,3},{2,4},{3,5},{4,6},{5,7},{6,0},{7,1},{8,10},{9,11},{10,... | collective-permute-start | bytes 3932168 | tf_op jit(solution)/shard_map/ppermute | solution.py:451
  70.0 174.1 %collective-permute-start.4 = (bf16[640,1024]{1,0:T(8,128)(2,1)S(1)}, bf16[640,1024]{1,0:T(8,128)(2,1)}, u32[]{:S(2)}, u32[]{:S(2)}) collective-permute-start(bf16[640,1024]{1,0:T(8,128)(2,1)S(1)} %unit.13), channel_id=1, source_target_pairs={{0,6},{1,7},{2,0},{3,1},{4,2},{5,3},{6,4},{7,5},{8,14},{9,15},{10,... | collective-permute-start | bytes 3932168 | tf_op jit(solution)/shard_map/ppermute | solution.py:451
  98.2 1.7 copy-start.1
  180.7 73.7 %collective-permute-start.5 = (bf16[640,1024]{1,0:T(8,128)(2,1)}, bf16[640,1024]{1,0:T(8,128)(2,1)}, u32[]{:S(2)}, u32[]{:S(2)}) collective-permute-start(bf16[640,1024]{1,0:T(8,128)(2,1)} %unit.14), channel_id=1, source_target_pairs={{0,1},{1,2},{2,3},{3,4},{4,5},{5,6},{6,7},{7,0},{8,9},{9,10},{10,1... | collective-permute-start | bytes 3932168 | tf_op jit(solution)/shard_map/ppermute | solution.py:451
  221.7 44.6 %collective-permute-start.6 = (bf16[640,1024]{1,0:T(8,128)(2,1)}, bf16[640,1024]{1,0:T(8,128)(2,1)}, u32[]{:S(2)}, u32[]{:S(2)}) collective-permute-start(bf16[640,1024]{1,0:T(8,128)(2,1)} %unit.15), channel_id=1, source_target_pairs={{0,7},{1,0},{2,1},{3,2},{4,3},{5,4},{6,5},{7,6},{8,15},{9,8},{10,9... | collective-permute-start | bytes 3932168 | tf_op jit(solution)/shard_map/ppermute | solution.py:451
Sparse Core Ops, SparseCore 0:
  45.8 45.5 reduce-scatter.2
  244.2 72.8 reduce-scatter.4
